TPU v7x, 32 devices: a whole 2x2x4 slice. The times are simulated.
32 devices in a mesh: chan: 8 (over z, x), ma: 4 (over y, core).
Axes of the slice: x: 2, y: 2, z: 4, core: 2. Of those that a mesh axis runs over, the one named last changes fastest.
Arguments:
- beam_table: bfloat16 [64, 1024, 2048], P(('ma', 'chan')), parts along dimension 0, may hold values from -0.125 to 0.125
- covariance: bfloat16 [8192, 16, 16], P(('ma', 'chan')), parts along dimension 0, as said below
- noise_var: float32 [64, 512], P(('ma', 'chan')), parts along dimension 0, may hold values from 0.5 to 4
- start_field: float32 [64, 512, 256], P(('ma', 'chan')), parts along dimension 0, may hold values from -4 to 4
- probes: float32 [64, 512, 256], P(('ma', 'chan')), parts along dimension 0, may hold values from -6 to 6
Outputs:
- solved: float32 [64, 512, 256], P(('ma', 'chan')), parts along dimension 0
- multipole_band_power: bfloat16 [8192, 16, 16], P(('ma', 'chan')), parts along dimension 0
There are 4 independent parts, one for each index of `ma`. A program takes and returns all parts, laid end to end along the dimension named above; each array names one. Nothing has to cross between parts.
Inputs may be any that keep to these rules, and one draw needn't show every extreme that they name: Each covariance[l] is symmetric with diagonal entries between 1 and 2.
All inputs are finite; a program needn't handle non-finite values.
Results may differ from a plain program's by a relative error of at most 0.009.
Values may be sent and summed in bfloat16 or wider, within the bound.
A program may use at most 128 MiB of HBM per device.

v0:
```python
import jax
import jax.numpy as jnp
from jax import lax
from jax.sharding import PartitionSpec as P

ITERS = 2


WEIGHT = 0.2


def project_back(beam_table, field_b):
    column_entries = field_b.shape[2] // 2
    reals = field_b[:, :, :column_entries]
    imags = field_b[:, :, column_entries:]
    lower = jnp.concatenate([imags, -reals], axis=2)
    stacked = jnp.concatenate([field_b, lower], axis=1)
    return jnp.einsum("fkl,fkc->flc", beam_table, stacked, preferred_element_type=jnp.float32)


def project_out(beam_table, mixed_back):
    column_entries = mixed_back.shape[2] // 2
    modes = beam_table.shape[1] // 2
    product = jnp.einsum("fkl,flc->fkc", beam_table, mixed_back, preferred_element_type=jnp.float32)
    upper = product[:, :modes]
    lower = product[:, modes:]
    return jnp.concatenate(
        [
            upper[:, :, :column_entries] - lower[:, :, column_entries:],
            upper[:, :, column_entries:] + lower[:, :, :column_entries],
        ],
        axis=2,
    )


def apply_operator(beam_table, covariance, field):
    field_b = field.astype(jnp.bfloat16)
    sky_map = project_back(beam_table, field_b).astype(jnp.bfloat16)
    channel_mixed = jnp.einsum(
        "drj,jdi->rdi",
        covariance,
        lax.all_to_all(sky_map, "chan", split_axis=1, concat_axis=0, tiled=True),
        preferred_element_type=jnp.float32,
    )
    mixed_back = lax.all_to_all(
        channel_mixed.astype(jnp.bfloat16), "chan", split_axis=0, concat_axis=1, tiled=True
    )
    return project_out(beam_table, mixed_back)


def on_device(beam_table, covariance, noise_var, start_field, probes):
    field = start_field
    column_entries = field.shape[2] // 2
    for repeat in range(ITERS):
        image = apply_operator(beam_table, covariance, field)
        field = field + WEIGHT * (probes - image - noise_var[:, :, None] * field)
    final_sky = project_back(beam_table, field.astype(jnp.bfloat16)).astype(jnp.bfloat16)
    collected_parts = lax.all_to_all(final_sky, "chan", split_axis=1, concat_axis=0, tiled=True)
    multipole_band_power = (
        jnp.einsum(
            "mjk,ujk->jmu", collected_parts, collected_parts, preferred_element_type=jnp.float32
        )
        / column_entries
    )
    return (field, multipole_band_power.astype(jnp.bfloat16))


def solution(mesh):
    return jax.shard_map(
        on_device,
        mesh=mesh,
        in_specs=(
            P(("ma", "chan"), None, None),
            P(("ma", "chan"), None, None),
            P(("ma", "chan"), None),
            P(("ma", "chan"), None, None),
            P(("ma", "chan"), None, None),
        ),
        out_specs=(P(("ma", "chan"), None, None), P(("ma", "chan"), None, None)),
        check_vma=False,
    )
```

profile of v0, /device:TPU:0, one launch (start us, length us, event | category | flops | bytes accessed | tf_op | source)
XLA Modules:
  0.0 362.4 jit_solution(10907388293487810081)
XLA Ops:
  2.3 5.9 %fusion = bf16[2,2048,256]{1,2,0:T(8,128)(2,1)S(1)} fusion(bf16[2,1024,2048]{2,1,0:T(8,128)(2,1)} %param.5, bf16[2,512,128]{1,2,0:T(8,128)(2,1)S(1)} %get-tuple-element.17, bf16[2,512,128]{1,2,0:T(8,128)(2,1)S(1)} %get-tuple-element.16, bf16[2,512,256]{1,2,0:T(8,128)(2,1)S(1)} %convert_element_type.42), kind=kOutput, calls=%fused_computation.3 | convolution fusion | flops 2151677952 | bytes 11534336 | tf_op jit(solution)/shard_map/fkl,fkc->flc/dot_general | solution.py:18
  8.2 3.9 %copy.22 = bf16[2,2048,256]{2,0,1:T(2,128)(2,1)} copy(bf16[2,2048,256]{1,2,0:T(8,128)(2,1)S(1)} %fusion) | data formatting | bytes 4194304 | tf_op jit(solution)/shard_map/convert_element_type | solution.py:38
  12.1 7.4 %all-to-all-start = ((bf16[2,2048,256]{2,0,1:T(2,128)(2,1)}), bf16[2,2048,256]{2,0,1:T(2,128)(2,1)}, u32[]{:S(2)}, u32[]{:S(2)}) async-start(bf16[2,2048,256]{2,0,1:T(2,128)(2,1)} %copy.22), calls=%async_computation | async-start | bytes 4194304 | tf_op jit(solution)/shard_map/all_to_all | solution.py:42
  20.4 47.4 %all-to-all-done = bf16[2,2048,256]{2,0,1:T(2,128)(2,1)} async-done(((bf16[2,2048,256]{2,0,1:T(2,128)(2,1)}), bf16[2,2048,256]{2,0,1:T(2,128)(2,1)}, u32[]{:S(2)}, u32[]{:S(2)}) %all-to-all-start) | async-done | bytes 2097184 | tf_op jit(solution)/shard_map/all_to_all | solution.py:42
  67.8 4.3 %copy.45 = bf16[2,8,256,256]{3,0,1,2:T(2,128)(2,1)} copy(bf16[2,8,256,256]{3,0,2,1:T(2,128)(2,1)} %bitcast.1) | data formatting | bytes 4194304 | tf_op jit(solution)/shard_map/all_to_all | solution.py:42
  72.1 4.1 %all_to_all.68 = bf16[16,256,256]{2,0,1:T(8,128)(2,1)} reshape(bf16[8,2,256,256]{3,1,0,2:T(2,128)(2,1)} %bitcast.58) | data formatting | bytes 4194304 | tf_op jit(solution)/shard_map/all_to_all | solution.py:42
  80.6 4.5 %all-to-all-start.1 = ((bf16[16,256,256]{2,1,0:T(8,128)(2,1)}), bf16[16,256,256]{2,1,0:T(8,128)(2,1)}, u32[]{:S(2)}, u32[]{:S(2)}) async-start(bf16[16,256,256]{2,1,0:T(8,128)(2,1)} %copy.25), calls=%async_computation.1 | async-start | bytes 4194304 | tf_op jit(solution)/shard_map/all_to_all | solution.py:45
  86.7 46.2 %all-to-all-done.1 = bf16[16,256,256]{2,1,0:T(8,128)(2,1)} async-done(((bf16[16,256,256]{2,1,0:T(8,128)(2,1)}), bf16[16,256,256]{2,1,0:T(8,128)(2,1)}, u32[]{:S(2)}, u32[]{:S(2)}) %all-to-all-start.1) | async-done | bytes 2097184 | tf_op jit(solution)/shard_map/all_to_all | solution.py:45
  132.8 4.5 %copy.26 = bf16[8,2,256,256]{2,0,3,1:T(8,128)(2,1)} copy(bf16[8,2,256,256]{3,2,1,0:T(8,128)(2,1)} %bitcast.4) | data formatting | bytes 4194304 | tf_op jit(solution)/shard_map/all_to_all | solution.py:45
  137.4 4.2 %all_to_all.72 = bf16[2,2048,256]{1,2,0:T(8,128)(2,1)} reshape(bf16[2,8,256,256]{2,1,3,0:T(8,128)(2,1)} %bitcast.59) | data formatting | bytes 4194304 | tf_op jit(solution)/shard_map/all_to_all | solution.py:45
  141.6 6.4 %convolution_bitcast_fusion.1 = f32[2,1024,256]{1,2,0:T(8,128)S(1)} fusion(bf16[2,2048,256]{1,2,0:T(8,128)(2,1)} %all_to_all.72, bf16[2,1024,2048]{2,1,0:T(8,128)(2,1)} %param.5), kind=kOutput, calls=%fused_computation.13 | convolution fusion | flops 2147483648 | bytes 12582912 | tf_op jit(solution)/shard_map/fkl,flc->fkc/dot_general | solution.py:24
  149.2 7.2 %fusion.1 = bf16[2,2048,256]{1,2,0:T(8,128)(2,1)} fusion(bf16[2,1024,2048]{2,1,0:T(8,128)(2,1)} %param.5, bf16[2,512,128]{1,2,0:T(8,128)(2,1)S(1)} %get-tuple-element.15, bf16[2,512,128]{1,2,0:T(8,128)(2,1)S(1)} %get-tuple-element.14, bf16[2,512,256]{1,2,0:T(8,128)(2,1)S(1)} %fusion.24), kind=kOutput, calls=%fused_computation.4 | convolution fusion | flops 2151677952 | bytes 11534336 | tf_op jit(solution)/shard_map/fkl,fkc->flc/dot_general | solution.py:18
  156.4 6.1 %copy.30 = bf16[2,2048,256]{2,0,1:T(2,128)(2,1)} copy(bf16[2,2048,256]{1,2,0:T(8,128)(2,1)} %fusion.1) | data formatting | bytes 4194304 | tf_op jit(solution)/shard_map/convert_element_type | solution.py:38
  162.5 51.9 %all_to_all.90 = bf16[2,2048,256]{2,0,1:T(2,128)(2,1)S(1)} all-to-all(bf16[2,2048,256]{2,0,1:T(2,128)(2,1)} %copy.30), channel_id=1, replica_groups=mesh['chan'=8,'ma'=4] {'chan'}, dimensions={1} | all-to-all | bytes 4194304 | tf_op jit(solution)/shard_map/all_to_all | solution.py:42
  214.4 2.8 copy.44
  217.2 4.1 %all_to_all.76 = bf16[16,256,256]{2,0,1:T(8,128)(2,1)} reshape(bf16[8,2,256,256]{3,1,0,2:T(2,128)(2,1)} %bitcast.61) | data formatting | bytes 4194304 | tf_op jit(solution)/shard_map/all_to_all | solution.py:42
  224.3 51.5 %all_to_all.91 = bf16[16,256,256]{2,1,0:T(8,128)(2,1)} all-to-all(bf16[16,256,256]{2,1,0:T(8,128)(2,1)S(1)} %copy.33), channel_id=1, replica_groups=mesh['chan'=8,'ma'=4] {'chan'}, dimensions={0} | all-to-all | bytes 4194304 | tf_op jit(solution)/shard_map/all_to_all | solution.py:45
  275.8 4.5 %copy.34 = bf16[8,2,256,256]{2,0,3,1:T(8,128)(2,1)} copy(bf16[8,2,256,256]{3,2,1,0:T(8,128)(2,1)} %bitcast.62) | data formatting | bytes 4194304 | tf_op jit(solution)/shard_map/all_to_all | solution.py:45
  280.3 4.2 %all_to_all.80 = bf16[2,2048,256]{1,2,0:T(8,128)(2,1)} reshape(bf16[2,8,256,256]{2,1,3,0:T(8,128)(2,1)} %bitcast.63) | data formatting | bytes 4194304 | tf_op jit(solution)/shard_map/all_to_all | solution.py:45
  284.5 6.4 %convolution_bitcast_fusion = f32[2,1024,256]{1,2,0:T(8,128)S(1)} fusion(bf16[2,2048,256]{1,2,0:T(8,128)(2,1)} %all_to_all.80, bf16[2,1024,2048]{2,1,0:T(8,128)(2,1)} %param.5), kind=kOutput, calls=%fused_computation.12 | convolution fusion | flops 2147483648 | bytes 12582912 | tf_op jit(solution)/shard_map/fkl,flc->fkc/dot_general | solution.py:24
  293.6 5.8 %fusion.2 = bf16[2,2048,256]{1,2,0:T(8,128)(2,1)S(1)} fusion(bf16[2,1024,2048]{2,1,0:T(8,128)(2,1)} %param.5, bf16[2,512,128]{1,2,0:T(8,128)(2,1)S(1)} %get-tuple-element.13, bf16[2,512,128]{1,2,0:T(8,128)(2,1)S(1)} %get-tuple-element.12, bf16[2,512,256]{1,2,0:T(8,128)(2,1)S(1)} %get-tuple-element.6), kind=kOutput, calls=%fused_computation.5 | convolution fusion | flops 2151677952 | bytes 11534336 | tf_op jit(solution)/shard_map/fkl,fkc->flc/dot_general | solution.py:18
  299.4 3.9 %copy.36 = bf16[2,2048,256]{2,0,1:T(2,128)(2,1)} copy(bf16[2,2048,256]{1,2,0:T(8,128)(2,1)S(1)} %fusion.2) | data formatting | bytes 4194304 | tf_op jit(solution)/shard_map/convert_element_type | solution.py:57
  303.3 3.7 %all-to-all-start.4 = ((bf16[2,2048,256]{2,0,1:T(2,128)(2,1)}), bf16[2,2048,256]{2,0,1:T(2,128)(2,1)S(1)}, u32[]{:S(2)}, u32[]{:S(2)}) async-start(bf16[2,2048,256]{2,0,1:T(2,128)(2,1)} %copy.36), calls=%async_computation.4 | async-start | bytes 4194304 | tf_op jit(solution)/shard_map/all_to_all | solution.py:58
  308.4 46.3 %all-to-all-done.4 = bf16[2,2048,256]{2,0,1:T(2,128)(2,1)S(1)} async-done(((bf16[2,2048,256]{2,0,1:T(2,128)(2,1)}), bf16[2,2048,256]{2,0,1:T(2,128)(2,1)S(1)}, u32[]{:S(2)}, u32[]{:S(2)}) %all-to-all-start.4) | async-done | bytes 2097184 | tf_op jit(solution)/shard_map/all_to_all | solution.py:58
  (34 shorter events, 24.3 us)
Async XLA Ops:
  12.0 7.4 %copy-start.5 = (bf16[256,16,16]{0,2,1:T(8,128)(2,1)S(1)}, bf16[256,16,16]{0,2,1:T(8,128)(2,1)}, u32[]{:S(2)}) copy-start(bf16[256,16,16]{0,2,1:T(8,128)(2,1)} %param.6) | copy-start | bytes 393220
  12.1 55.7 %all-to-all-start = ((bf16[2,2048,256]{2,0,1:T(2,128)(2,1)}), bf16[2,2048,256]{2,0,1:T(2,128)(2,1)}, u32[]{:S(2)}, u32[]{:S(2)}) async-start(bf16[2,2048,256]{2,0,1:T(2,128)(2,1)} %copy.22), calls=%async_computation | async-start | bytes 4194304 | tf_op jit(solution)/shard_map/all_to_all | solution.py:42
  80.6 52.3 %all-to-all-start.1 = ((bf16[16,256,256]{2,1,0:T(8,128)(2,1)}), bf16[16,256,256]{2,1,0:T(8,128)(2,1)}, u32[]{:S(2)}, u32[]{:S(2)}) async-start(bf16[16,256,256]{2,1,0:T(8,128)(2,1)} %copy.25), calls=%async_computation.1 | async-start | bytes 4194304 | tf_op jit(solution)/shard_map/all_to_all | solution.py:45
  148.0 0.7 copy-start.6
  148.2 0.9 copy-start
  148.2 1.0 copy-start.2
  290.9 1.0 copy-start.1
  290.9 1.2 copy-start.3
  303.3 3.7 %copy-start.4 = (f32[2,512,256]{1,2,0:T(8,128)S(1)}, f32[2,512,256]{1,2,0:T(8,128)}, u32[]{:S(2)}) copy-start(f32[2,512,256]{1,2,0:T(8,128)} %get-tuple-element.7) | copy-start | bytes 3145732
  303.3 51.4 %all-to-all-start.4 = ((bf16[2,2048,256]{2,0,1:T(2,128)(2,1)}), bf16[2,2048,256]{2,0,1:T(2,128)(2,1)S(1)}, u32[]{:S(2)}, u32[]{:S(2)}) async-start(bf16[2,2048,256]{2,0,1:T(2,128)(2,1)} %copy.36), calls=%async_computation.4 | async-start | bytes 4194304 | tf_op jit(solution)/shard_map/all_to_all | solution.py:58
where the time goes:
time: 364 us; the launch traced here: 362 us
  waiting for transfers between devices  140 us (38%)
  blocking collectives  103 us (28%)
  local copies, waits for them, and re-layouts  63.3 us (17%)
  matrix products  36.8 us (10%)
  starting transfers between devices  15.7 us (4%)
    all_to_all x1, blocking collectives, apply_operator(): lax.all_to_all(sky_map, 'chan', split_axis=1, concat_axis=0, tiled=True)  51.9 us
    all_to_all x1, blocking collectives, apply_operator(): lax.all_to_all(channel_mixed.astype(jnp.bfloat16), 'chan', split_axis=0,...  51.5 us
    all_to_all x1, waiting for transfers between devices, apply_operator(): lax.all_to_all(sky_map, 'chan', split_axis=1, concat_axis=0, tiled=True)  47.4 us
    all_to_all x1, waiting for transfers between devices, on_device(): lax.all_to_all(final_sky, 'chan', split_axis=1, concat_axis=0, tiled=True)  46.3 us
    all_to_all x1, waiting for transfers between devices, apply_operator(): lax.all_to_all(channel_mixed.astype(jnp.bfloat16), 'chan', split_axis=0,...  46.2 us
    dot_general x3, matrix products, project_back(): jnp.einsum('fkl,fkc->flc', beam_table, stacked, preferred_element_type=jn...  18.9 us
    all_to_all x4, local copies, waits for them, and re-layouts, apply_operator(): lax.all_to_all(channel_mixed.astype(jnp.bfloat16), 'chan', split_axis=0,...  17.5 us
    all_to_all x4, local copies, waits for them, and re-layouts, apply_operator(): lax.all_to_all(sky_map, 'chan', split_axis=1, concat_axis=0, tiled=True)  15.4 us
  transfers between devices with their start and end apart: 3, of which 3 were waited for; matrix products, arithmetic and copies ran while one was open for 1% of the time, Pallas kernels for 0%

commit v1 on v0

--- a/solution.py
+++ b/solution.py
@@ -1,12 +1,297 @@
+import functools
+
 import jax
 import jax.numpy as jnp
 from jax import lax
+from jax.experimental import pallas as pl
+from jax.experimental.pallas import tpu as pltpu
 from jax.sharding import PartitionSpec as P
 
 ITERS = 2
 
 
 WEIGHT = 0.2
+
+GROUP = 16
+PIECES = 2
+
+
+def kernel(
+    beam_hbm, cov_ref, noise_ref, start_ref, probes_ref, solved_ref, power_ref,
+    beam, beam_t, stacked, product, diag, sky, skies, mixed, back,
+    load_sem, out_send, out_recv, back_send, back_recv,
+):
+    channels, modes, columns = start_ref.shape
+    half = columns // 2
+    owners = back.shape[2]
+    rows = back.shape[4]
+    owned = PIECES * rows
+    groups = rows // GROUP
+    block = GROUP * channels * owners
+    me = lax.axis_index("chan")
+
+    def partner(d):
+        place = 0
+        for bit in (4, 2, 1):
+            mine = lax.rem(lax.div(me, bit), 2)
+            flip = lax.rem(lax.div(jnp.int32(d), jnp.int32(bit)), jnp.int32(2))
+            place = place + bit * (mine + flip - 2 * mine * flip)
+        return place
+
+    def load(d):
+        cols = pl.ds(pl.multiple_of(partner(d) * owned, 128), owned)
+        return pltpu.make_async_copy(
+            beam_hbm.at[:, :, cols], beam.at[:, :, cols], load_sem.at[d]
+        )
+
+    def send_sky(it, s, d):
+        return pltpu.make_async_remote_copy(
+            src_ref=sky.at[s, d],
+            dst_ref=skies.at[it, s, pl.ds(channels * me, channels)],
+            send_sem=out_send.at[it, s, d],
+            recv_sem=out_recv.at[it, s, d],
+            device_id={"chan": partner(d)},
+            device_id_type=pl.DeviceIdType.MESH,
+        )
+
+    def send_mixed(it, s, d):
+        to = partner(d)
+        return pltpu.make_async_remote_copy(
+            src_ref=mixed.at[s, pl.ds(channels * to, channels)],
+            dst_ref=back.at[it, s, me],
+            send_sem=back_send.at[it, s, d],
+            recv_sem=back_recv.at[it, s, d],
+            device_id={"chan": to},
+            device_id_type=pl.DeviceIdType.MESH,
+        )
+
+    def each(body):
+        def step(i, carry):
+            body(owners - 1 - i)
+            return carry
+
+        lax.fori_loop(0, owners - 1, step, 0)
+
+    def start_load(d):
+        load(d).start()
+
+    each(start_load)
+    load(0).start()
+
+    barrier = pltpu.get_barrier_semaphore()
+
+    def greet(d):
+        pl.semaphore_signal(
+            barrier, inc=1, device_id={"chan": partner(d)},
+            device_id_type=pl.DeviceIdType.MESH,
+        )
+
+    each(greet)
+
+    row = lax.broadcasted_iota(jnp.int32, (block, block), 0)
+    col = lax.broadcasted_iota(jnp.int32, (block, block), 1)
+    same = lax.rem(row, GROUP) == lax.rem(col, GROUP)
+    width = cov_ref.shape[2]
+    spread_row = lax.broadcasted_iota(jnp.int32, (width, block), 0)
+    spread_col = lax.broadcasted_iota(jnp.int32, (width, block), 1)
+    pick_row = lax.broadcasted_iota(jnp.int32, (block, width), 0)
+    pick_col = lax.broadcasted_iota(jnp.int32, (block, width), 1)
+    per_group = block // GROUP
+
+    def stack(field):
+        for ch in range(channels):
+            values = field[ch].astype(jnp.bfloat16)
+            stacked[ch, 0:modes, :] = values
+            stacked[ch, modes : 2 * modes, 0:half] = values[:, half:]
+            stacked[ch, modes : 2 * modes, half:] = -values[:, :half]
+
+    def project(it, s, d, own):
+        l0 = pl.multiple_of(partner(d) * owned + s * rows, 128)
+        if it == 0 and s == 0:
+            load(d).wait()
+        for ch in range(channels):
+            if it == 0:
+                tile = beam[ch, :, pl.ds(l0, rows)].T
+                beam_t[ch, pl.ds(l0, rows), :] = tile
+            else:
+                tile = beam_t[ch, pl.ds(l0, rows), :]
+            value = jnp.dot(
+                tile, stacked[ch], preferred_element_type=jnp.float32
+            ).astype(jnp.bfloat16)
+            if own:
+                skies[it, s, channels * me + ch] = value
+            else:
+                sky[s, d, ch] = value
+
+    def send_all(it):
+        for s in range(PIECES):
+            def step(d):
+                project(it, s, d, False)
+                send_sky(it, s, d).start()
+
+            each(step)
+        for s in range(PIECES):
+            project(it, s, 0, True)
+
+    def mix(it, s):
+        def arrive(d):
+            send_sky(it, s, d).wait_recv()
+
+        each(arrive)
+
+        def step(q, carry):
+            r0 = pl.multiple_of(q * GROUP, GROUP)
+            x = skies[it, s, :, pl.ds(r0, GROUP), :].reshape(block, columns)
+            y = jnp.dot(diag[s, q], x, preferred_element_type=jnp.float32)
+            mixed[s, :, pl.ds(r0, GROUP), :] = y.astype(jnp.bfloat16).reshape(
+                per_group, GROUP, columns
+            )
+            return carry
+
+        lax.fori_loop(0, groups, step, 0)
+
+        def reply(d):
+            send_mixed(it, s, d).start()
+
+        each(reply)
+
+    def add_image(it, s, d, own):
+        owner = partner(d)
+        l0 = pl.multiple_of(owner * owned + s * rows, 128)
+        for ch in range(channels):
+            if own:
+                values = mixed[s, channels * me + ch]
+            else:
+                values = back[it, s, owner, ch]
+            term = jnp.dot(
+                beam[ch, :, pl.ds(l0, rows)], values,
+                preferred_element_type=jnp.float32,
+            )
+            if own and s == 0:
+                product[ch] = term
+            else:
+                product[ch] += term
+
+    stack(start_ref)
+    pl.semaphore_wait(barrier, owners - 1)
+
+    for it in range(ITERS):
+        send_all(it)
+        if it == 0:
+            for s in range(PIECES):
+                def fill(q, carry):
+                    spread = jnp.where(
+                        spread_row == q * per_group + lax.div(spread_col, GROUP),
+                        1.0, 0.0,
+                    ).astype(jnp.bfloat16)
+                    wide = jnp.dot(
+                        cov_ref[s], spread, preferred_element_type=jnp.float32
+                    )
+                    diag[s, q] = jnp.where(same, wide, 0.0).astype(jnp.bfloat16)
+                    return carry
+
+                lax.fori_loop(0, groups, fill, 0)
+        for s in range(PIECES):
+            mix(it, s)
+        for s in range(PIECES):
+            add_image(it, s, 0, True)
+        for s in range(PIECES):
+            def collect(d):
+                send_mixed(it, s, d).wait_recv()
+                add_image(it, s, d, False)
+                send_sky(it, s, d).wait_send()
+
+            each(collect)
+        for s in range(PIECES):
+            def sent(d):
+                send_mixed(it, s, d).wait_send()
+
+            each(sent)
+        field = start_ref if it == 0 else solved_ref
+        for ch in range(channels):
+            upper = product[ch, 0:modes, :]
+            lower = product[ch, modes : 2 * modes, :]
+            image = jnp.concatenate(
+                [upper[:, :half] - lower[:, half:], upper[:, half:] + lower[:, :half]],
+                axis=1,
+            )
+            old = field[ch]
+            solved_ref[ch] = old + WEIGHT * (
+                probes_ref[ch] - image - noise_ref[ch] * old
+            )
+        stack(solved_ref)
+
+    send_all(ITERS)
+    for s in range(PIECES):
+        def arrive(d):
+            send_sky(ITERS, s, d).wait_recv()
+
+        each(arrive)
+
+        def power(q, total):
+            r0 = pl.multiple_of(q * GROUP, GROUP)
+            x = skies[ITERS, s, :, pl.ds(r0, GROUP), :].reshape(block, columns)
+            gram = lax.dot_general(
+                x, x, (((1,), (1,)), ((), ())), preferred_element_type=jnp.float32
+            )
+            kept = jnp.where(same, gram / half, 0.0).astype(jnp.bfloat16)
+            pick = jnp.where(
+                pick_col == q * per_group + lax.div(pick_row, GROUP), 1.0, 0.0
+            ).astype(jnp.bfloat16)
+            return total + jnp.dot(kept, pick, preferred_element_type=jnp.float32)
+
+        total = lax.fori_loop(
+            0, groups, power, jnp.zeros((block, width), jnp.float32)
+        )
+        power_ref[s] = total.astype(jnp.bfloat16)
+    for s in range(PIECES):
+        def gone(d):
+            send_sky(ITERS, s, d).wait_send()
+
+        each(gone)
+
+
+def fused(owners, beam_table, covariance, noise_var, start_field, probes):
+    channels, modes, columns = start_field.shape
+    owned, every, _ = covariance.shape
+    rows = owned // PIECES
+    groups = rows // GROUP
+    block = GROUP * every
+    cov = covariance.reshape(PIECES, groups, GROUP, every, every)
+    cov = cov.transpose(0, 3, 2, 1, 4).reshape(PIECES, block, groups * every)
+    vmem = pl.BlockSpec(memory_space=pltpu.VMEM)
+    bf16 = jnp.bfloat16
+    dma = pltpu.SemaphoreType.DMA
+    solved, power = pl.pallas_call(
+        kernel,
+        out_shape=(
+            jax.ShapeDtypeStruct(start_field.shape, jnp.float32),
+            jax.ShapeDtypeStruct(cov.shape, bf16),
+        ),
+        in_specs=[pl.BlockSpec(memory_space=pl.ANY)] + [vmem] * 4,
+        out_specs=(vmem, vmem),
+        scratch_shapes=[
+            pltpu.VMEM(beam_table.shape, bf16),
+            pltpu.VMEM((channels, owned * owners, 2 * modes), bf16),
+            pltpu.VMEM((channels, 2 * modes, columns), bf16),
+            pltpu.VMEM((channels, 2 * modes, columns), jnp.float32),
+            pltpu.VMEM((PIECES, groups, block, block), bf16),
+            pltpu.VMEM((PIECES, owners, channels, rows, columns), bf16),
+            pltpu.VMEM((ITERS + 1, PIECES, every, rows, columns), bf16),
+            pltpu.VMEM((PIECES, every, rows, columns), bf16),
+            pltpu.VMEM((ITERS, PIECES, owners, channels, rows, columns), bf16),
+            dma((owners,)),
+            dma((ITERS + 1, PIECES, owners)),
+            dma((ITERS + 1, PIECES, owners)),
+            dma((ITERS, PIECES, owners)),
+            dma((ITERS, PIECES, owners)),
+        ],
+        compiler_params=pltpu.CompilerParams(
+            collective_id=0, has_side_effects=True, vmem_limit_bytes=56 * 2**20
+        ),
+    )(beam_table, cov, noise_var[:, :, None], start_field, probes)
+    power = power.reshape(PIECES, every, GROUP, groups, every)
+    return solved, power.transpose(0, 3, 2, 1, 4).reshape(covariance.shape)
 
 
 def project_back(beam_table, field_b):
@@ -48,7 +333,19 @@
     return project_out(beam_table, mixed_back)
 
 
-def on_device(beam_table, covariance, noise_var, start_field, probes):
+def fits(owners, beam_table, covariance):
+    owned, every, _ = covariance.shape
+    return (
+        owners == 8
+        and every * GROUP == 256
+        and owned % (128 * PIECES) == 0
+        and beam_table.size <= 4 * 2**20
+    )
+
+
+def on_device(owners, beam_table, covariance, noise_var, start_field, probes):
+    if fits(owners, beam_table, covariance):
+        return fused(owners, beam_table, covariance, noise_var, start_field, probes)
     field = start_field
     column_entries = field.shape[2] // 2
     for repeat in range(ITERS):
@@ -67,7 +364,7 @@
 
 def solution(mesh):
     return jax.shard_map(
-        on_device,
+        functools.partial(on_device, mesh.shape["chan"]),
         mesh=mesh,
         in_specs=(
             P(("ma", "chan"), None, None),

time: 364 us -> 256 us (0.70)
  Pallas kernels: 0 us -> 242 us
  waiting for transfers between devices: 140 us -> 0 us
  blocking collectives: 103 us -> 0 us
  local copies, waits for them, and re-layouts: 63.3 us -> 12.8 us
  matrix products: 36.8 us -> 0 us
  starting transfers between devices: 15.7 us -> 0 us
    pallas_call x0 -> x1, Pallas kernels: none -> 242 us  [fused(): pl.pallas_call(kernel, out_shape=(jax.ShapeDtypeStruct(start_field.shape,...]
    all_to_all x3 -> x0, waiting for transfers between devices: 140 us -> none  [the longest x1 47.4 us: apply_operator(): lax.all_to_all(sky_map, 'chan', split_axis=1, concat_axis=0, tiled=True)]
    all_to_all x2 -> x0, blocking collectives: 103 us -> none  [the longest x1 51.9 us: apply_operator(): lax.all_to_all(sky_map, 'chan', split_axis=1, concat_axis=0, tiled=True)]
    all_to_all x10 -> x0, local copies, waits for them, and re-layouts: 38.4 us -> none  [the longest x4 17.5 us: apply_operator(): lax.all_to_all(channel_mixed.astype(jnp.bfloat16), 'chan', split_axis=0,...]
    dot_general x8 -> x0, matrix products: 36.8 us -> none  [the longest x3 18.9 us: project_back(): jnp.einsum('fkl,fkc->flc', beam_table, stacked, preferred_element_type=jn...]
    convert_element_type x5 -> x0, local copies, waits for them, and re-layouts: 16.6 us -> none  [the longest x2 10 us: apply_operator(): sky_map = project_back(beam_table, field_b).astype(jnp.bfloat16)]
    all_to_all x3 -> x0, starting transfers between devices: 15.7 us -> none  [the longest x1 7.39 us: apply_operator(): lax.all_to_all(sky_map, 'chan', split_axis=1, concat_axis=0, tiled=True)]
    reshape x0 -> x5, local copies, waits for them, and re-layouts: none -> 7.62 us  [the longest x2 2.88 us: fused(): cov = covariance.reshape(PIECES, groups, GROUP, every, every)]
  transfers between devices with their start and end apart: 3 -> 0, of which waited for: 3 -> 0; matrix products, arithmetic and copies ran while one was open for 1% -> 0% of each run, Pallas kernels for 0% -> 0%
where the time goes in v1:
time: 256 us; the launch traced here: 255 us
  Pallas kernels  242 us (95%)
  local copies, waits for them, and re-layouts  12.8 us (5%)
    pallas_call x1, Pallas kernels, fused(): pl.pallas_call(kernel, out_shape=(jax.ShapeDtypeStruct(start_field.shape,...  242 us

profile of v1, /device:TPU:0, one launch (start us, length us, event | category | flops | bytes accessed | tf_op | source)
XLA Modules:
  0.0 255.4 jit_solution(14914592935328140590)
XLA Ops:
  0.6 1.7 copy.10.noise_ref
  2.3 1.8 reshape.16
  4.1 1.1 copy.9
  5.2 1.3 reshape.17.cov_ref
  6.6 241.9 %shard_map.68 = (f32[2,512,256]{2,1,0:T(8,128)}, bf16[2,256,128]{2,1,0:T(8,128)(2,1)}) custom-call(bf16[2,1024,2048]{2,1,0:T(8,128)(2,1)} %beam_hbm.1, bf16[2,256,128]{2,1,0:T(8,128)(2,1)} %reshape.17.cov_ref, f32[2,512,1]{2,1,0:T(8,128)} %copy.10.noise_ref, f32[2,512,256]{2,1,0:T(8,128)} %start_ref.1, f32[2,512,256]{2,1,0:T(8,128)} %probes_ref.1), custom_call_target="tpu_custom_call" | custom-call | tf_op jit(solution)/shard_map/pallas_call | solution.py:265
  248.5 1.8 reshape.18
  250.2 1.2 copy.11
  251.5 1.7 reshape.19
  253.1 2.3 copy.13

commit v2 on v1

--- a/solution.py
+++ b/solution.py
@@ -18,7 +18,7 @@
 
 def kernel(
     beam_hbm, cov_ref, noise_ref, start_ref, probes_ref, solved_ref, power_ref,
-    beam, beam_t, stacked, product, diag, sky, skies, mixed, back,
+    beam, beam_t, stacked, product, diag, sky, skies, mixed, back, noise,
     load_sem, out_send, out_recv, back_send, back_recv,
 ):
     channels, modes, columns = start_ref.shape
@@ -72,6 +72,13 @@
 
         lax.fori_loop(0, owners - 1, step, 0)
 
+    def nearest(body):
+        def step(i, carry):
+            body(i + 1)
+            return carry
+
+        lax.fori_loop(0, owners - 1, step, 0)
+
     def start_load(d):
         load(d).start()
 
@@ -91,11 +98,14 @@
     row = lax.broadcasted_iota(jnp.int32, (block, block), 0)
     col = lax.broadcasted_iota(jnp.int32, (block, block), 1)
     same = lax.rem(row, GROUP) == lax.rem(col, GROUP)
-    width = cov_ref.shape[2]
-    spread_row = lax.broadcasted_iota(jnp.int32, (width, block), 0)
-    spread_col = lax.broadcasted_iota(jnp.int32, (width, block), 1)
-    pick_row = lax.broadcasted_iota(jnp.int32, (block, width), 0)
-    pick_col = lax.broadcasted_iota(jnp.int32, (block, width), 1)
+    across = lax.rem(row, GROUP) == lax.div(col, GROUP)
+    alike = jnp.where(lax.div(row, GROUP) == lax.div(col, GROUP), 1.0, 0.0).astype(
+        jnp.bfloat16
+    )
+    spot_row = lax.broadcasted_iota(jnp.int32, (owned, block), 0)
+    spot_col = lax.broadcasted_iota(jnp.int32, (owned, block), 1)
+    place_row = lax.broadcasted_iota(jnp.int32, (block, owned), 0)
+    place_col = lax.broadcasted_iota(jnp.int32, (block, owned), 1)
     per_group = block // GROUP
 
     def stack(field):
@@ -133,6 +143,22 @@
         for s in range(PIECES):
             project(it, s, 0, True)
 
+    def fill(s):
+        table = cov_ref[...].reshape(block, owned)
+
+        def step(q, carry):
+            base = s * rows + q * GROUP
+            spot = jnp.where(
+                spot_row == base + lax.rem(spot_col, GROUP), 1.0, 0.0
+            ).astype(jnp.bfloat16)
+            wide = jnp.dot(table, spot, preferred_element_type=jnp.float32)
+            wide = jnp.where(across, wide, 0.0).astype(jnp.bfloat16)
+            wide = jnp.dot(alike, wide, preferred_element_type=jnp.float32)
+            diag[s, q] = jnp.where(same, wide, 0.0).astype(jnp.bfloat16)
+            return carry
+
+        lax.fori_loop(0, groups, step, 0, unroll=2)
+
     def mix(it, s):
         def arrive(d):
             send_sky(it, s, d).wait_recv()
@@ -148,7 +174,7 @@
             )
             return carry
 
-        lax.fori_loop(0, groups, step, 0)
+        lax.fori_loop(0, groups, step, 0, unroll=True)
 
         def reply(d):
             send_mixed(it, s, d).start()
@@ -178,20 +204,13 @@
     for it in range(ITERS):
         send_all(it)
         if it == 0:
-            for s in range(PIECES):
-                def fill(q, carry):
-                    spread = jnp.where(
-                        spread_row == q * per_group + lax.div(spread_col, GROUP),
-                        1.0, 0.0,
-                    ).astype(jnp.bfloat16)
-                    wide = jnp.dot(
-                        cov_ref[s], spread, preferred_element_type=jnp.float32
-                    )
-                    diag[s, q] = jnp.where(same, wide, 0.0).astype(jnp.bfloat16)
-                    return carry
-
-                lax.fori_loop(0, groups, fill, 0)
-        for s in range(PIECES):
+            for ch in range(channels):
+                noise[ch] = jnp.broadcast_to(
+                    noise_ref[ch : ch + 1, :], (half, modes)
+                ).T
+        for s in range(PIECES):
+            if it == 0:
+                fill(s)
             mix(it, s)
         for s in range(PIECES):
             add_image(it, s, 0, True)
@@ -201,7 +220,7 @@
                 add_image(it, s, d, False)
                 send_sky(it, s, d).wait_send()
 
-            each(collect)
+            nearest(collect)
         for s in range(PIECES):
             def sent(d):
                 send_mixed(it, s, d).wait_send()
@@ -217,11 +236,12 @@
             )
             old = field[ch]
             solved_ref[ch] = old + WEIGHT * (
-                probes_ref[ch] - image - noise_ref[ch] * old
+                probes_ref[ch] - image - jnp.concatenate([noise[ch], noise[ch]], axis=1) * old
             )
         stack(solved_ref)
 
     send_all(ITERS)
+    total = jnp.zeros((block, owned), jnp.float32)
     for s in range(PIECES):
         def arrive(d):
             send_sky(ITERS, s, d).wait_recv()
@@ -235,15 +255,15 @@
                 x, x, (((1,), (1,)), ((), ())), preferred_element_type=jnp.float32
             )
             kept = jnp.where(same, gram / half, 0.0).astype(jnp.bfloat16)
-            pick = jnp.where(
-                pick_col == q * per_group + lax.div(pick_row, GROUP), 1.0, 0.0
+            kept = jnp.dot(alike, kept, preferred_element_type=jnp.float32)
+            kept = jnp.where(across, kept, 0.0).astype(jnp.bfloat16)
+            place = jnp.where(
+                place_col == s * rows + q * GROUP + lax.rem(place_row, GROUP), 1.0, 0.0
             ).astype(jnp.bfloat16)
-            return total + jnp.dot(kept, pick, preferred_element_type=jnp.float32)
-
-        total = lax.fori_loop(
-            0, groups, power, jnp.zeros((block, width), jnp.float32)
-        )
-        power_ref[s] = total.astype(jnp.bfloat16)
+            return total + jnp.dot(kept, place, preferred_element_type=jnp.float32)
+
+        total = lax.fori_loop(0, groups, power, total, unroll=True)
+    power_ref[...] = total.astype(jnp.bfloat16).reshape(power_ref.shape)
     for s in range(PIECES):
         def gone(d):
             send_sky(ITERS, s, d).wait_send()
@@ -257,8 +277,7 @@
     rows = owned // PIECES
     groups = rows // GROUP
     block = GROUP * every
-    cov = covariance.reshape(PIECES, groups, GROUP, every, every)
-    cov = cov.transpose(0, 3, 2, 1, 4).reshape(PIECES, block, groups * every)
+    cov = covariance.transpose(1, 2, 0)
     vmem = pl.BlockSpec(memory_space=pltpu.VMEM)
     bf16 = jnp.bfloat16
     dma = pltpu.SemaphoreType.DMA
@@ -280,6 +299,7 @@
             pltpu.VMEM((ITERS + 1, PIECES, every, rows, columns), bf16),
             pltpu.VMEM((PIECES, every, rows, columns), bf16),
             pltpu.VMEM((ITERS, PIECES, owners, channels, rows, columns), bf16),
+            pltpu.VMEM((channels, modes, columns // 2), jnp.float32),
             dma((owners,)),
             dma((ITERS + 1, PIECES, owners)),
             dma((ITERS + 1, PIECES, owners)),
@@ -289,9 +309,8 @@
         compiler_params=pltpu.CompilerParams(
             collective_id=0, has_side_effects=True, vmem_limit_bytes=56 * 2**20
         ),
-    )(beam_table, cov, noise_var[:, :, None], start_field, probes)
-    power = power.reshape(PIECES, every, GROUP, groups, every)
-    return solved, power.transpose(0, 3, 2, 1, 4).reshape(covariance.shape)
+    )(beam_table, cov, noise_var, start_field, probes)
+    return solved, power.transpose(2, 0, 1)
 
 
 def project_back(beam_table, field_b):

time: 256 us -> 246 us (0.961)
  local copies, waits for them, and re-layouts: 12.8 us -> 3.83 us
    reshape x5 -> x0, local copies, waits for them, and re-layouts: 7.62 us -> none  [the longest x2 2.88 us: fused(): cov = covariance.reshape(PIECES, groups, GROUP, every, every)]
where the time goes in v2:
time: 246 us
  Pallas kernels  242 us (98%)
  local copies, waits for them, and re-layouts  3.83 us (2%)
    pallas_call x1, Pallas kernels, fused(): pl.pallas_call(kernel, out_shape=(jax.ShapeDtypeStruct(start_field.shape,...  242 us

profile of v2, /device:TPU:0, one launch (start us, length us, event | category | flops | bytes accessed | tf_op | source)
XLA Modules:
  0.0 246.0 jit_solution(18105695879315768208)
XLA Ops:
  0.6 241.5 %shard_map.68 = (f32[2,512,256]{2,1,0:T(8,128)}, bf16[16,16,256]{2,1,0:T(8,128)(2,1)}) custom-call(bf16[2,1024,2048]{2,1,0:T(8,128)(2,1)} %beam_hbm.1, bf16[16,16,256]{2,1,0:T(8,128)(2,1)} %bitcast.2, f32[2,512]{1,0:T(2,128)} %noise_ref.1, f32[2,512,256]{2,1,0:T(8,128)} %start_ref.1, f32[2,512,256]{2,1,0:T(8,128)} %probes_ref.1), custom_call_target="tpu_custom_call" | custom-call | tf_op jit(solution)/shard_map/pallas_call | solution.py:284
  242.2 2.3 copy.9
  244.4 1.6 copy.10

commit v3 on v2

--- a/solution.py
+++ b/solution.py
@@ -269,6 +269,11 @@
             send_sky(ITERS, s, d).wait_send()
 
         each(gone)
+
+
+def hand_over(solved_ref, power_ref, solved_out, power_out):
+    solved_out[...] = solved_ref[...]
+    power_out[...] = power_ref[...]
 
 
 def fused(owners, beam_table, covariance, noise_var, start_field, probes):
@@ -310,6 +315,15 @@
             collective_id=0, has_side_effects=True, vmem_limit_bytes=56 * 2**20
         ),
     )(beam_table, cov, noise_var, start_field, probes)
+    solved, power = pl.pallas_call(
+        hand_over,
+        out_shape=(
+            jax.ShapeDtypeStruct(solved.shape, solved.dtype),
+            jax.ShapeDtypeStruct(power.shape, power.dtype),
+        ),
+        in_specs=[vmem] * 2,
+        out_specs=(vmem, vmem),
+    )(solved, power)
     return solved, power.transpose(2, 0, 1)
 
 

time: 246 us -> 245 us (level)
  local copies, waits for them, and re-layouts: 3.83 us -> 0 us
    unnamed x2 -> x0, local copies, waits for them, and re-layouts: 3.83 us -> none
where the time goes in v3:
time: 245 us; the launch traced here: 244 us
  Pallas kernels  244 us (100%)
    pallas_call x1, Pallas kernels, fused(): pl.pallas_call(kernel, out_shape=(jax.ShapeDtypeStruct(start_field.shape,...  242 us

profile of v3, /device:TPU:0, one launch (start us, length us, event | category | flops | bytes accessed | tf_op | source)
XLA Modules:
  0.0 244.5 jit_solution(13395766627056463605)
XLA Ops:
  0.6 241.5 %shard_map.68 = (f32[2,512,256]{2,1,0:T(8,128)}, bf16[16,16,256]{2,1,0:T(8,128)(2,1)}) custom-call(bf16[2,1024,2048]{2,1,0:T(8,128)(2,1)} %beam_hbm.1, bf16[16,16,256]{2,1,0:T(8,128)(2,1)} %bitcast.2, f32[2,512]{1,0:T(2,128)} %noise_ref.1, f32[2,512,256]{2,1,0:T(8,128)} %start_ref.1, f32[2,512,256]{2,1,0:T(8,128)} %probes_ref.1), custom_call_target="tpu_custom_call" | custom-call | tf_op jit(solution)/shard_map/pallas_call | solution.py:289
  242.2 2.3 shard_map.69
